TPU v7x, 32 devices: a whole 2x2x4 slice. The times are simulated.
32 devices in a mesh: group: 2 (over y), samp: 4 (over z), site: 2 (over x), sub: 2 (over core).
Axes of the slice: x: 2, y: 2, z: 4, core: 2. Of those that a mesh axis runs over, the one named last changes fastest.
Arguments:
- points: bfloat16 [1280, 16384], P(('group', 'samp'), ('site', 'sub')), parts along dimension 0, may hold values from -6 to 6
- scores: bfloat16 [1280, 16384], P(('group', 'samp'), ('site', 'sub')), parts along dimension 0, may hold values from -6 to 6
- target: bfloat16 [1280], P(('group', 'samp')), parts along dimension 0, may hold values from -6 to 13.5
Outputs:
- coeff: float32 [1280], P(('group', 'samp')), parts along dimension 0
- residual: float32 [1280], P(('group', 'samp')), parts along dimension 0
There are 2 independent parts, one for each index of `group`. A program takes and returns all parts, laid end to end along the dimension named above; each array names one. Nothing has to cross between parts.
All inputs are finite; a program needn't handle non-finite values.
Results may differ from a plain program's by a relative error of at most 0.0003.
Values may be sent and summed in bfloat16 or wider, within the bound.
A program may use at most 64 MiB of HBM per device.

v0:
```python
import jax
import jax.numpy as jnp
from jax import lax
from jax.sharding import PartitionSpec as P

SITES = 16384


RIDGE = 0.5


def from_behind(value, axis, steps):
    count = lax.axis_size(axis)
    pairs = [(source, (source + steps) % count) for source in range(count)]
    return lax.ppermute(value, axis, pairs)


def partial_tiles(own_points, own_scores, vis_points, vis_scores):
    spec = (((1,), (1,)), ((), ()))
    gram = lax.dot_general(own_points, vis_points, spec, preferred_element_type=jnp.float32)
    score_gram = lax.dot_general(own_scores, vis_scores, spec, preferred_element_type=jnp.float32)
    return (gram, score_gram)


def stein_block(gram, score_gram, row_norms, col_norms, width):
    sq_dist = row_norms[:, None] + col_norms[None, :] - 2.0 * gram
    return jnp.exp(-sq_dist / (2.0 * width)) * (score_gram + 1.0) / width


def kernel_rows(own_points, own_scores, vis_points, vis_scores, row_norms, col_norms, width):
    parts = partial_tiles(own_points, own_scores, vis_points, vis_scores)
    gram, score_gram = lax.psum((parts[0], parts[1]), ("site", "sub"))
    return stein_block(gram, score_gram, row_norms, col_norms, width)


def body(points, scores, target):
    count = points.shape[0]
    width = float(SITES)
    highest = lax.Precision.HIGHEST
    values = target.astype(jnp.float32)
    norm_sq = lax.psum(jnp.sum(values * values), "samp")
    self_sq = jnp.einsum("ik,ik->i", points, points, preferred_element_type=jnp.float32)
    own_norms = lax.psum(self_sq, ("site", "sub"))
    every_norms = lax.all_gather(own_norms, "samp", axis=0, tiled=True)
    cycle_size = lax.axis_size("samp")
    position = lax.axis_index("samp")

    def visitor_norms(step):
        owner = (position - step) % cycle_size
        return lax.dynamic_slice_in_dim(every_norms, owner * count, count, 0)

    block = kernel_rows(points, scores, points, scores, own_norms, own_norms, width)
    image = jnp.dot(block, values, precision=highest)
    owed = None
    half = cycle_size // 2

    def half_step(step, carry):
        vis_points, vis_scores, vis_target, carried, image_now = carry
        vis_points, vis_scores, vis_target = from_behind(
            (vis_points, vis_scores, vis_target), "samp", 1
        )
        tile = kernel_rows(
            points, scores, vis_points, vis_scores, own_norms, visitor_norms(step), width
        )
        image_now = image_now + jnp.dot(tile, vis_target.astype(jnp.float32), precision=highest)
        carried = carried + jnp.dot(values, tile, precision=highest)
        carried = from_behind(carried, "samp", 1)
        return (vis_points, vis_scores, vis_target, carried, image_now)

    start = (points, scores, target, jnp.zeros((count,), jnp.float32), image)
    vis_points, vis_scores, vis_target, carried, image = lax.fori_loop(1, half, half_step, start)
    owed = from_behind(carried, "samp", -half)
    vis_points, vis_scores, vis_target = from_behind(
        (vis_points, vis_scores, vis_target), "samp", 1
    )
    tile = kernel_rows(
        points, scores, vis_points, vis_scores, own_norms, visitor_norms(half), width
    )
    image = image + jnp.dot(tile, vis_target.astype(jnp.float32), precision=highest)
    image = image + owed
    image = image + RIDGE * values
    curvature = lax.psum(jnp.sum(values * image), "samp")
    alpha = norm_sq / curvature
    return (alpha * values, values - alpha * image)


def solution(mesh):
    return jax.shard_map(
        body,
        mesh=mesh,
        in_specs=(
            P(("group", "samp"), ("site", "sub")),
            P(("group", "samp"), ("site", "sub")),
            P(("group", "samp")),
        ),
        out_specs=(P(("group", "samp")), P(("group", "samp"))),
        check_vma=False,
    )
```

profile of v0, /device:TPU:0, one launch (start us, length us, event | category | flops | bytes accessed | tf_op | source)
XLA Modules:
  0.0 195.6 jit_solution(1652588069864532109)
XLA Ops:
  7.2 0.0 copy-start.3
  7.2 0.0 copy-start
  7.2 0.0 all-reduce.5.cloned.1.call-start
  7.2 3.1 %collective-permute-start.1 = (bf16[160,4096]{1,0:T(8,128)(2,1)}, bf16[160,4096]{1,0:T(8,128)(2,1)}, u32[]{:S(2)}, u32[]{:S(2)}) collective-permute-start(bf16[160,4096]{1,0:T(8,128)(2,1)} %param.4), channel_id=1, source_target_pairs={{0,4},{4,8},{8,12},{12,0},{1,5},{5,9},{9,13},{13,1},{2,6},{6,10},{... | collective-permute-start | bytes 3932168 | tf_op jit(solution)/shard_map/while/body/eval_jaxpr/ppermute | solution.py:15
  10.3 1.6 collective-permute-start
  11.9 30.4 %collective-permute-done.1 = bf16[160,4096]{1,0:T(8,128)(2,1)} collective-permute-done((bf16[160,4096]{1,0:T(8,128)(2,1)}, bf16[160,4096]{1,0:T(8,128)(2,1)}, u32[]{:S(2)}, u32[]{:S(2)}) %collective-permute-start.1) | collective-permute-done | bytes 1310752 | tf_op jit(solution)/shard_map/while/body/eval_jaxpr/ppermute | solution.py:15
  42.3 0.0 collective-permute-start.4
  42.3 1.6 collective-permute-start.2
  43.9 26.4 %collective-permute-done = bf16[160,4096]{1,0:T(8,128)(2,1)S(1)} collective-permute-done((bf16[160,4096]{1,0:T(8,128)(2,1)}, bf16[160,4096]{1,0:T(8,128)(2,1)S(1)}, u32[]{:S(2)}, u32[]{:S(2)}) %collective-permute-start) | collective-permute-done | bytes 1310752 | tf_op jit(solution)/shard_map/while/body/eval_jaxpr/ppermute | solution.py:15
  70.2 0.0 collective-permute-start.3
  70.3 2.9 %fusion.47 = f32[160,160]{1,0:T(8,128)} fusion(bf16[160,4096]{1,0:T(8,128)(2,1)} %param.4), kind=kOutput, calls=%fused_computation.53 | convolution fusion | flops 209715200 | bytes 1413120 | tf_op jit(solution)/shard_map/dot_general | solution.py:21
  73.1 0.0 copy-done.3
  73.2 0.6 dynamic-slice
  74.4 0.0 copy-done
  74.4 0.0 copy-start.1
  74.4 1.2 fusion.46
  75.6 0.1 copy-done.1
  75.7 2.5 %fusion.49 = f32[160,160]{1,0:T(8,128)} fusion(bf16[160,4096]{1,0:T(8,128)(2,1)S(1)} %copy-done.1, bf16[160,4096]{1,0:T(8,128)(2,1)} %collective-permute-done.1), kind=kOutput, calls=%fused_computation.55 | convolution fusion | flops 209715200 | bytes 2723840 | tf_op jit(solution)/shard_map/while/body/eval_jaxpr/dot_general | solution.py:21
  78.2 1.2 fusion.48
  79.4 19.0 %collective-permute-done.4 = bf16[160,4096]{1,0:T(8,128)(2,1)} collective-permute-done((bf16[160,4096]{1,0:T(8,128)(2,1)}, bf16[160,4096]{1,0:T(8,128)(2,1)}, u32[]{:S(2)}, u32[]{:S(2)}) %collective-permute-start.4) | collective-permute-done | bytes 1310752 | tf_op jit(solution)/shard_map/ppermute | solution.py:15
  98.4 2.5 %fusion.52 = f32[160,160]{1,0:T(8,128)} fusion(bf16[160,4096]{1,0:T(8,128)(2,1)S(1)} %copy-done.1, bf16[160,4096]{1,0:T(8,128)(2,1)} %collective-permute-done.4), kind=kOutput, calls=%fused_computation.58 | convolution fusion | flops 209715200 | bytes 2723840 | tf_op jit(solution)/shard_map/dot_general | solution.py:21
  100.9 24.8 %collective-permute-done.3 = bf16[160,4096]{1,0:T(8,128)(2,1)} collective-permute-done((bf16[160,4096]{1,0:T(8,128)(2,1)S(1)}, bf16[160,4096]{1,0:T(8,128)(2,1)}, u32[]{:S(2)}, u32[]{:S(2)}) %collective-permute-start.3) | collective-permute-done | bytes 1310752 | tf_op jit(solution)/shard_map/ppermute | solution.py:15
  125.7 2.5 %fusion.51 = f32[160,160]{1,0:T(8,128)} fusion(bf16[160,4096]{1,0:T(8,128)(2,1)S(1)} %copy-done, bf16[160,4096]{1,0:T(8,128)(2,1)} %collective-permute-done.3), kind=kOutput, calls=%fused_computation.57 | convolution fusion | flops 209715200 | bytes 2723840 | tf_op jit(solution)/shard_map/dot_general | solution.py:20
  128.2 0.0 copy-start.2
  128.2 0.0 all-reduce.5.cloned.1.call-update
  128.2 0.3 fusion
  128.6 5.8 %psum.66 = f32[160]{0:T(256)S(1)} all-reduce(f32[160]{0:T(256)S(1)} %fusion), channel_id=1, replica_groups=mesh['group'=2,'samp'=4,'site'=2,'sub'=2] {'site','sub'}, use_global_device_ids=true, to_apply=%region_2.0 | all-reduce | flops 160 | bytes 1280 | tf_op jit(solution)/shard_map/psum | solution.py:43
  134.3 0.2 dynamic-update-slice
  134.6 10.0 %all-reduce = f32[640]{0:T(1024)S(1)} all-reduce(f32[640]{0:T(1024)S(1)} %dynamic-update-slice), channel_id=1, replica_groups=mesh['group'=2,'samp'=4,'site'=2,'sub'=2] {'samp'}, use_global_device_ids=true, to_apply=%add | all-reduce | flops 640 | bytes 5120
  144.6 0.0 collective-permute-done.2
  144.6 0.4 collective-permute-start.5
  145.0 0.1 fusion.45
  145.0 0.0 copy-done.2
  145.0 4.9 %collective-permute-done.5 = bf16[160]{0:T(256)(128)(2,1)S(1)} collective-permute-done((bf16[160]{0:T(256)(128)(2,1)S(1)}, bf16[160]{0:T(256)(128)(2,1)S(1)}, u32[]{:S(2)}, u32[]{:S(2)}) %collective-permute-start.5) | collective-permute-done | bytes 352 | tf_op jit(solution)/shard_map/ppermute | solution.py:15
  150.0 14.6 %all-reduce.5.cloned.1.call-done = (f32[160,160]{1,0:T(8,128)}, f32[160,160]{1,0:T(8,128)}, f32[160,160]{1,0:T(8,128)}, f32[160,160]{1,0:T(8,128)}, f32[160,160]{1,0:T(8,128)}, /*index=5*/f32[160,160]{1,0:T(8,128)}) async-done(((f32[160,160]{1,0:T(8,128)}, f32[160,160]{1,0:T(8,128)}, f32[160,160]{1,0:T(8,128)}, f32[160,160]{1,0:T(8,128)}, f32[160,160]{1,0:T(8,128)}, /*index=5*/f32[160,160]{1,0:T(8,128)}), ...) | async-done | bytes 614416 | tf_op jit(solution)/shard_map/while/body/eval_jaxpr/psum | solution.py:32
  164.6 1.1 multiply_multiply_fusion
  165.7 0.2 fusion.53
  165.9 1.5 collective-permute-start.6
  167.4 1.2 fusion.11
  168.6 1.3 fusion.1
  169.9 1.3 collective-permute-done.6
  171.2 1.2 collective-permute-start.7
  172.4 0.2 fusion.50
  172.6 3.1 %collective-permute-done.7 = f32[160]{0:T(256)S(1)} collective-permute-done((f32[160]{0:T(256)S(1)}, f32[160]{0:T(256)S(1)}, u32[]{:S(2)}, u32[]{:S(2)}) %collective-permute-start.7) | collective-permute-done | bytes 672 | tf_op jit(solution)/shard_map/ppermute | solution.py:15
  175.7 0.6 fusion.35
  176.3 10.5 %all-reduce.2 = (f32[]{:T(128)}, f32[]{:T(128)}) all-reduce(f32[]{:T(128)} %get-tuple-element.29, f32[]{:T(128)} %get-tuple-element.28), channel_id=1, replica_groups=mesh['group'=2,'samp'=4,'site'=2,'sub'=2] {'samp'}, use_global_device_ids=true, to_apply=%region_1.0 | all-reduce | flops 2 | bytes 16 | tf_op jit(solution)/shard_map/psum | solution.py:41
  188.1 0.6 convert_subtract_fusion
  (4 shorter events, 0.0 us)
Async XLA Ops:
  7.2 66.0 %copy-start.3 = (u32[32]{0:T(128)S(1)}, u32[32]{0:T(128)}, u32[]{:S(2)}) copy-start(u32[32]{0:T(128)} %constant.73) | copy-start | bytes 388
  7.2 67.2 %copy-start = (bf16[160,4096]{1,0:T(8,128)(2,1)S(1)}, bf16[160,4096]{1,0:T(8,128)(2,1)}, u32[]{:S(2)}) copy-start(bf16[160,4096]{1,0:T(8,128)(2,1)} %param.3) | copy-start | bytes 3932164
  7.2 157.4 %all-reduce.5.cloned.1.call-start = ((), (), s32[]{:S(2)}) async-start(), calls=%async_computation | async-start | bytes 1966080 | tf_op jit(solution)/shard_map/while/body/eval_jaxpr/psum | solution.py:32
  7.2 35.0 %collective-permute-start.1 = (bf16[160,4096]{1,0:T(8,128)(2,1)}, bf16[160,4096]{1,0:T(8,128)(2,1)}, u32[]{:S(2)}, u32[]{:S(2)}) collective-permute-start(bf16[160,4096]{1,0:T(8,128)(2,1)} %param.4), channel_id=1, source_target_pairs={{0,4},{4,8},{8,12},{12,0},{1,5},{5,9},{9,13},{13,1},{2,6},{6,10},{... | collective-permute-start | bytes 3932168 | tf_op jit(solution)/shard_map/while/body/eval_jaxpr/ppermute | solution.py:15
  10.3 59.9 %collective-permute-start = (bf16[160,4096]{1,0:T(8,128)(2,1)}, bf16[160,4096]{1,0:T(8,128)(2,1)S(1)}, u32[]{:S(2)}, u32[]{:S(2)}) collective-permute-start(bf16[160,4096]{1,0:T(8,128)(2,1)} %param.3), channel_id=1, source_target_pairs={{0,4},{4,8},{8,12},{12,0},{1,5},{5,9},{9,13},{13,1},{2,6},{6,10},{... | collective-permute-start | bytes 3932168 | tf_op jit(solution)/shard_map/while/body/eval_jaxpr/ppermute | solution.py:15
  42.3 56.2 %collective-permute-start.4 = (bf16[160,4096]{1,0:T(8,128)(2,1)}, bf16[160,4096]{1,0:T(8,128)(2,1)}, u32[]{:S(2)}, u32[]{:S(2)}) collective-permute-start(bf16[160,4096]{1,0:T(8,128)(2,1)} %collective-permute-done.1), channel_id=1, source_target_pairs={{0,4},{4,8},{8,12},{12,0},{1,5},{5,9},{9,13},{13,1},{2,6},{6,10},{... | collective-permute-start | bytes 3932168 | tf_op jit(solution)/shard_map/ppermute | solution.py:15
  42.3 102.3 %collective-permute-start.2 = (bf16[160]{0:T(256)(128)(2,1)}, bf16[160]{0:T(256)(128)(2,1)S(1)}, u32[]{:S(2)}, u32[]{:S(2)}) collective-permute-start(bf16[160]{0:T(256)(128)(2,1)} %param.5), channel_id=1, source_target_pairs={{0,4},{4,8},{8,12},{12,0},{1,5},{5,9},{9,13},{13,1},{2,6},{6,10},{... | collective-permute-start | bytes 968 | tf_op jit(solution)/shard_map/while/body/eval_jaxpr/ppermute | solution.py:15
  70.2 55.5 %collective-permute-start.3 = (bf16[160,4096]{1,0:T(8,128)(2,1)S(1)}, bf16[160,4096]{1,0:T(8,128)(2,1)}, u32[]{:S(2)}, u32[]{:S(2)}) collective-permute-start(bf16[160,4096]{1,0:T(8,128)(2,1)S(1)} %collective-permute-done), channel_id=1, source_target_pairs={{0,4},{4,8},{8,12},{12,0},{1,5},{5,9},{9,13},{13,1},{2,6},{6,10},{... | collective-permute-start | bytes 3932168 | tf_op jit(solution)/shard_map/ppermute | solution.py:15
  74.4 1.3 copy-start.1
  128.2 16.8 %copy-start.2 = (bf16[160]{0:T(256)(128)(2,1)S(1)}, bf16[160]{0:T(256)(128)(2,1)}, u32[]{:S(2)}) copy-start(bf16[160]{0:T(256)(128)(2,1)} %param.5) | copy-start | bytes 964
  144.6 5.4 %collective-permute-start.5 = (bf16[160]{0:T(256)(128)(2,1)S(1)}, bf16[160]{0:T(256)(128)(2,1)S(1)}, u32[]{:S(2)}, u32[]{:S(2)}) collective-permute-start(bf16[160]{0:T(256)(128)(2,1)S(1)} %collective-permute-done.2), channel_id=1, source_target_pairs={{0,4},{4,8},{8,12},{12,0},{1,5},{5,9},{9,13},{13,1},{2,6},{6,10},{... | collective-permute-start | bytes 968 | tf_op jit(solution)/shard_map/ppermute | solution.py:15
  165.9 5.4 %collective-permute-start.6 = (f32[160]{0:T(256)S(1)}, f32[160]{0:T(256)S(1)}, u32[]{:S(2)}, u32[]{:S(2)}) collective-permute-start(f32[160]{0:T(256)S(1)} %bitcast.26), channel_id=1, source_target_pairs={{0,4},{4,8},{8,12},{12,0},{1,5},{5,9},{9,13},{13,1},{2,6},{6,10},{... | collective-permute-start | bytes 1928 | tf_op jit(solution)/shard_map/while/body/eval_jaxpr/ppermute | solution.py:15
  171.2 4.5 %collective-permute-start.7 = (f32[160]{0:T(256)S(1)}, f32[160]{0:T(256)S(1)}, u32[]{:S(2)}, u32[]{:S(2)}) collective-permute-start(f32[160]{0:T(256)S(1)} %collective-permute-done.6), channel_id=1, source_target_pairs={{0,8},{4,12},{8,0},{12,4},{1,9},{5,13},{9,1},{13,5},{2,10},{6,14},... | collective-permute-start | bytes 1928 | tf_op jit(solution)/shard_map/ppermute | solution.py:15
Sparse Core Ops, SparseCore 0:
  128.3 36.1 all-reduce.4
where the time goes:
time: 196 us
  waiting for transfers between devices  125 us (64%)
  blocking collectives  26.3 us (13%)
  between operations  16.1 us (8%)
  matrix products  15.6 us (8%)
  starting transfers between devices  9.35 us (5%)
  other arithmetic  2.63 us (1%)
    ppermute x8, waiting for transfers between devices, from_behind(): return lax.ppermute(value, axis, pairs)  110 us
    psum x1, waiting for transfers between devices, kernel_rows(): gram, score_gram = lax.psum((parts[0], parts[1]), ('site', 'sub'))  14.6 us
    psum x1, blocking collectives, body(): norm_sq = lax.psum(jnp.sum(values * values), 'samp')  10.5 us
    unnamed x1, blocking collectives  9.99 us
    ppermute x8, starting transfers between devices, from_behind(): return lax.ppermute(value, axis, pairs)  9.31 us
    dot_general x3, matrix products, partial_tiles(): lax.dot_general(own_scores, vis_scores, spec, preferred_element_type=jnp....  7.87 us
    psum x1, blocking collectives, body(): own_norms = lax.psum(self_sq, ('site', 'sub'))  5.78 us
    dot_general x3, matrix products, partial_tiles(): lax.dot_general(own_points, vis_points, spec, preferred_element_type=jnp....  4.85 us
  transfers between devices with their start and end apart: 9, of which 8 were waited for; matrix products, arithmetic and copies ran while one was open for 9% of the time, Pallas kernels for 0%

commit v1 on v0

--- a/solution.py
+++ b/solution.py
@@ -1,6 +1,10 @@
+import functools
+
 import jax
 import jax.numpy as jnp
 from jax import lax
+from jax.experimental import pallas as pl
+from jax.experimental.pallas import tpu as pltpu
 from jax.sharding import PartitionSpec as P
 
 SITES = 16384
@@ -33,7 +37,7 @@
     return stein_block(gram, score_gram, row_norms, col_norms, width)
 
 
-def body(points, scores, target):
+def ring_body(points, scores, target):
     count = points.shape[0]
     width = float(SITES)
     highest = lax.Precision.HIGHEST
@@ -84,7 +88,391 @@
     return (alpha * values, values - alpha * image)
 
 
+MESH = pl.DeviceIdType.MESH
+LANES = 128
+F32 = jnp.float32
+
+
+def spread(col, row_ids, col_ids):
+    return jnp.sum(jnp.where(row_ids == col_ids, col, 0.0), axis=0, keepdims=True)
+
+
+def stand(row, row_ids, col_ids):
+    return jnp.sum(jnp.where(row_ids == col_ids, row, 0.0), axis=1, keepdims=True)
+
+
+def ids(n):
+    return (
+        lax.broadcasted_iota(jnp.int32, (n, n), 0),
+        lax.broadcasted_iota(jnp.int32, (n, n), 1),
+    )
+
+
+def fused_kernel(
+    nz,
+    points,
+    scores,
+    target,
+    coeff,
+    residual,
+    gathered,
+    own_points,
+    tiles,
+    core_in,
+    samp_in,
+    piece,
+    site_in,
+    vec_out,
+    vec_in,
+    img_out,
+    img_in,
+    norm_col,
+    value_col,
+    image_col,
+    norm_row,
+    value_row,
+    local_sem,
+    data_send,
+    data_recv,
+    vec_send,
+    vec_recv,
+    img_send,
+    img_recv,
+    core_sem,
+    samp_send,
+    samp_recv,
+    site_sem,
+):
+    z = lax.axis_index("samp")
+    x = lax.axis_index("site")
+    c = lax.axis_index("sub")
+    peers = 4 * nz
+    me = (c * nz + z) * 2 + x
+    count = target.shape[1]
+    total = nz * count
+    nb = total // LANES
+    span = points.shape[1] // nz
+    share = LANES // 2
+    rows = share // nz
+    half = rows // 2
+
+    def where(p):
+        return {"sub": p // (2 * nz), "samp": (p // 2) % nz, "site": p % 2}
+
+    barrier = pltpu.get_barrier_semaphore()
+    for k in range(1, peers):
+        pl.semaphore_signal(
+            barrier, inc=1, device_id=where((me + k) % peers), device_id_type=MESH
+        )
+    pl.semaphore_wait(barrier, peers - 1)
+
+    def strip(kind, to):
+        ref = points if kind == 0 else scores
+        return ref.at[:, pl.ds(pl.multiple_of(span * to, span), span)]
+
+    def slot(source_z, source_x):
+        return gathered.at[
+            source_x, pl.ds(pl.multiple_of(count * source_z, count), count), :
+        ]
+
+    def send_data(kind, to, number):
+        return pltpu.make_async_remote_copy(
+            src_ref=strip(kind, to),
+            dst_ref=slot(z, x),
+            send_sem=data_send.at[number],
+            recv_sem=data_recv.at[z, x],
+            device_id={"samp": to, "site": kind},
+            device_id_type=MESH,
+        )
+
+    order = [(z + nz // 2) % nz] + [(z + k) % nz for k in range(1, nz) if k != nz // 2]
+    if nz == 4:
+        order = [(z + 2) % 4, 3 - z, z + 1 - 2 * (z % 2)]
+    sends = []
+    for to in order:
+        for kind in (0, 1):
+            sends.append(send_data(kind, to, len(sends)))
+            sends[-1].start()
+
+    def same_chip(kind):
+        keep = pltpu.make_async_copy(strip(kind, z), slot(z, x), local_sem.at[1])
+        give = send_data(1 - kind, z, 2 * nz - 2)
+        return keep, give
+
+    for kind in (0, 1):
+
+        @pl.when(x == kind)
+        def _():
+            for copy in same_chip(kind):
+                copy.start()
+
+    fetch = pltpu.make_async_copy(points, own_points, local_sem.at[0])
+    fetch.start()
+    fetch.wait()
+    wide = 512
+    self_sq = jnp.zeros((count, 1), F32)
+    for k in range(points.shape[1] // wide):
+        part = own_points[:, wide * k : wide * (k + 1)].astype(F32)
+        self_sq = self_sq + jnp.sum(part * part, axis=1, keepdims=True)
+    row_ids, col_ids = ids(count)
+    eye_row, eye_col = ids(LANES)
+    vec_out[...] = jnp.zeros_like(vec_out)
+    vec_out[0:1, 0:count] = spread(self_sq, row_ids, col_ids)
+    vec_out[1:2, 0:count] = target[...]
+
+    def send_vec(source, to, number):
+        return pltpu.make_async_remote_copy(
+            src_ref=vec_out,
+            dst_ref=vec_in.at[source],
+            send_sem=vec_send.at[number],
+            recv_sem=vec_recv.at[source],
+            device_id=where(to),
+            device_id_type=MESH,
+        )
+
+    for k in range(1, peers):
+        send_vec(me, (me + k) % peers, k - 1).start()
+    vec_in[me] = vec_out[...]
+    for k in range(1, peers):
+        send_vec((me + k) % peers, (me + k) % peers, k - 1).wait_recv()
+    for k in range(nz):
+        norms = jnp.zeros((1, count), F32)
+        for i in range(2):
+            for j in range(2):
+                norms = norms + vec_in[(i * nz + k) * 2 + j, 0:1, 0:count]
+        values = vec_in[2 * k, 1:2, 0:count]
+        block = pl.ds(k * count, count)
+        norm_col[block, :] = jnp.broadcast_to(stand(norms, row_ids, col_ids), (count, LANES))
+        value_col[block, :] = jnp.broadcast_to(stand(values, row_ids, col_ids), (count, LANES))
+    norm_row[...] = jnp.zeros_like(norm_row)
+    value_row[...] = jnp.zeros_like(value_row)
+    for b in range(nb):
+        block = pl.ds(b * LANES, LANES)
+        norm_row[b : b + 1, :] = spread(norm_col[block, :], eye_row, eye_col)
+        value_row[b : b + 1, :] = spread(value_col[block, :], eye_row, eye_col)
+
+    def arrival(source_z, source_x):
+        return pltpu.make_async_remote_copy(
+            src_ref=slot(source_z, source_x),
+            dst_ref=slot(source_z, source_x),
+            send_sem=data_send.at[0],
+            recv_sem=data_recv.at[source_z, source_x],
+            device_id={"samp": source_z, "site": 1 - x},
+            device_id_type=MESH,
+        )
+
+    pltpu.make_async_copy(slot(z, x), slot(z, x), local_sem.at[1]).wait()
+    arrival(z, 1 - x).wait_recv()
+    for k in range(1, nz):
+        for j in (0, 1):
+            arrival((z + k) % nz, j).wait_recv()
+
+    pairs = [(i, j) for i in range(nb) for j in range(i, nb)]
+    for i in range(nb):
+        panel = jnp.zeros((LANES, total - LANES * i), F32)
+        for j in (0, 1):
+            panel = panel + lax.dot_general(
+                gathered[j, LANES * i : LANES * (i + 1), :],
+                gathered[j, LANES * i : total, :],
+                (((1,), (1,)), ((), ())),
+                preferred_element_type=F32,
+            )
+        for j in range(i, nb):
+            tiles[pairs.index((i, j))] = panel[:, LANES * (j - i) : LANES * (j - i + 1)]
+
+    mine = pl.ds(pl.multiple_of(share * c, share), share)
+    theirs = pl.ds(pl.multiple_of(share * (1 - c), share), share)
+    to_core = pltpu.make_async_remote_copy(
+        src_ref=tiles.at[:, theirs, :],
+        dst_ref=core_in,
+        send_sem=core_sem.at[0],
+        recv_sem=core_sem.at[1],
+        device_id={"sub": 1 - c},
+        device_id_type=MESH,
+    )
+    to_core.start()
+    to_core.wait_recv()
+    core_in[...] = core_in[...] + tiles[:, mine, :]
+
+    def send_piece(source, to, number):
+        return pltpu.make_async_remote_copy(
+            src_ref=core_in.at[:, pl.ds(pl.multiple_of(rows * to, rows), rows), :],
+            dst_ref=samp_in.at[source],
+            send_sem=samp_send.at[number],
+            recv_sem=samp_recv.at[source],
+            device_id={"samp": to},
+            device_id_type=MESH,
+        )
+
+    for number, to in enumerate(order):
+        send_piece(z, to, number).start()
+    samp_in[z] = core_in[:, pl.ds(pl.multiple_of(rows * z, rows), rows), :]
+    for k in range(1, nz):
+        send_piece((z + k) % nz, (z + k) % nz, 0).wait_recv()
+    summed = samp_in[0]
+    for k in range(1, nz):
+        summed = summed + samp_in[k]
+    piece[...] = summed
+
+    to_site = pltpu.make_async_remote_copy(
+        src_ref=piece.at[:, pl.ds(pl.multiple_of(half * (1 - x), half), half), :],
+        dst_ref=site_in,
+        send_sem=site_sem.at[0],
+        recv_sem=site_sem.at[1],
+        device_id={"site": 1 - x},
+        device_id_type=MESH,
+    )
+    to_site.start()
+    to_site.wait_recv()
+    here = piece[:, pl.ds(pl.multiple_of(half * x, half), half), :]
+    there = site_in[...]
+    gram = jnp.where(x == 0, here, there)
+    score_gram = jnp.where(x == 0, there, here)
+
+    width = float(SITES)
+    lane = lax.broadcasted_iota(jnp.int32, (half, LANES), 1)
+    over = [jnp.zeros((1, LANES), F32) for _ in range(nb)]
+    down = jnp.zeros((half, LANES), F32)
+    for i in range(nb):
+        at = pl.ds(pl.multiple_of(LANES * i + share * c + rows * z + half * x, half), half)
+        row_norms, row_values = norm_col[at, :], value_col[at, :]
+        for j in range(i, nb):
+            n = pairs.index((i, j))
+            sq_dist = row_norms + norm_row[j : j + 1, :] - 2.0 * gram[n]
+            kernel = jnp.exp(-sq_dist / (2.0 * width)) * (score_gram[n] + 1.0) / width
+            over[j] = over[j] + jnp.sum(kernel * row_values, axis=0, keepdims=True)
+            if j > i:
+                terms = jnp.sum(kernel * value_row[j : j + 1, :], axis=1, keepdims=True)
+                down = down + jnp.where(lane == i, terms, 0.0)
+    img_out[...] = jnp.zeros_like(img_out)
+    for j in range(nb):
+        img_out[j : j + 1, :] = over[j]
+    img_out[8 : 8 + half, :] = down
+
+    def send_img(source, to, number):
+        return pltpu.make_async_remote_copy(
+            src_ref=img_out,
+            dst_ref=img_in.at[source],
+            send_sem=img_send.at[number],
+            recv_sem=img_recv.at[source],
+            device_id=where(to),
+            device_id_type=MESH,
+        )
+
+    for k in range(1, peers):
+        send_img(me, (me + k) % peers, k - 1).start()
+    img_in[me] = img_out[...]
+    for k in range(1, peers):
+        send_img((me + k) % peers, (me + k) % peers, k - 1).wait_recv()
+    across = img_in[0, 0:8, :]
+    for p in range(1, peers):
+        across = across + img_in[p, 0:8, :]
+    below = jnp.concatenate([img_in[p, 8 : 8 + half, :] for p in range(peers)], axis=0)
+    curvature = jnp.zeros((1, 1), F32)
+    norm_sq = jnp.zeros((1, 1), F32)
+    for i in range(nb):
+        values = value_row[i : i + 1, :]
+        image = across[i : i + 1, :] + spread(below[:, i : i + 1], eye_row, eye_col)
+        image = image + RIDGE * values
+        curvature = curvature + jnp.sum(values * image, axis=1, keepdims=True)
+        norm_sq = norm_sq + jnp.sum(values * values, axis=1, keepdims=True)
+        image_col[LANES * i : LANES * (i + 1), :] = jnp.broadcast_to(
+            stand(image, eye_row, eye_col), (LANES, LANES)
+        )
+    alpha = norm_sq / curvature
+    own = image_col[pl.ds(pl.multiple_of(count * z, count), count), 0:1]
+    own_image = spread(own, row_ids, col_ids)
+    coeff[...] = alpha * target[...]
+    residual[...] = target[...] - alpha * own_image
+
+    for copy in sends:
+        copy.wait_send()
+    send_data(0, z, 2 * nz - 2).wait_send()
+    for k in range(1, peers):
+        send_vec(me, (me + k) % peers, k - 1).wait_send()
+        send_img(me, (me + k) % peers, k - 1).wait_send()
+    to_core.wait_send()
+    to_site.wait_send()
+    for number, to in enumerate(order):
+        send_piece(z, to, number).wait_send()
+
+
+def fused_body(nz, points, scores, target):
+    count, sites = points.shape
+    total = nz * count
+    nb = total // LANES
+    blocks = nb * (nb + 1) // 2
+    rows = LANES // 2 // nz
+    peers = 4 * nz
+    dma = pltpu.SemaphoreType.DMA
+    vmem = pl.BlockSpec(memory_space=pltpu.VMEM)
+    wide = -(-count // LANES) * LANES
+    coeff, residual = pl.pallas_call(
+        functools.partial(fused_kernel, nz),
+        out_shape=[jax.ShapeDtypeStruct((1, count), F32)] * 2,
+        in_specs=[pl.BlockSpec(memory_space=pl.ANY)] * 2 + [vmem],
+        out_specs=[vmem, vmem],
+        scratch_shapes=[
+            pltpu.VMEM((2, total, sites // nz), points.dtype),
+            pltpu.VMEM((count, sites), points.dtype),
+            pltpu.VMEM((blocks, LANES, LANES), F32),
+            pltpu.VMEM((blocks, LANES // 2, LANES), F32),
+            pltpu.VMEM((nz, blocks, rows, LANES), F32),
+            pltpu.VMEM((blocks, rows, LANES), F32),
+            pltpu.VMEM((blocks, rows // 2, LANES), F32),
+            pltpu.VMEM((8, wide), F32),
+            pltpu.VMEM((peers, 8, wide), F32),
+            pltpu.VMEM((16, LANES), F32),
+            pltpu.VMEM((peers, 16, LANES), F32),
+            pltpu.VMEM((total, LANES), F32),
+            pltpu.VMEM((total, LANES), F32),
+            pltpu.VMEM((total, LANES), F32),
+            pltpu.VMEM((8, LANES), F32),
+            pltpu.VMEM((8, LANES), F32),
+            dma((2,)),
+            dma((2 * nz - 1,)),
+            dma((nz, 2)),
+            dma((peers - 1,)),
+            dma((peers,)),
+            dma((peers - 1,)),
+            dma((peers,)),
+            dma((2,)),
+            dma((nz - 1,)),
+            dma((nz,)),
+            dma((2,)),
+        ],
+        compiler_params=pltpu.CompilerParams(
+            collective_id=0, has_side_effects=True, vmem_limit_bytes=40 * 2**20
+        ),
+        cost_estimate=pl.CostEstimate(
+            flops=2 * total * total * sites // 2,
+            bytes_accessed=4 * count * sites,
+            transcendentals=0,
+        ),
+    )(points, scores, target.astype(F32).reshape(1, count))
+    return coeff.reshape(count), residual.reshape(count)
+
+
 def solution(mesh):
+    sizes = dict(mesh.shape)
+
+    def body(points, scores, target):
+        nz = sizes["samp"]
+        total = nz * points.shape[0]
+        fits = (
+            sizes["site"] == 2
+            and sizes["sub"] == 2
+            and nz == 4
+            and points.shape[0] % 16 == 0
+            and total % LANES == 0
+            and total <= 8 * LANES
+            and points.shape[1] % (nz * LANES) == 0
+            and points.shape[1] % 512 == 0
+        )
+        if fits:
+            return fused_body(nz, points, scores, target)
+        return ring_body(points, scores, target)
+
     return jax.shard_map(
         body,
         mesh=mesh,

time: 196 us -> 97.4 us (0.50)
  waiting for transfers between devices: 125 us -> 0 us
  Pallas kernels: 0 us -> 92.2 us
  blocking collectives: 26.3 us -> 0 us
  matrix products: 15.6 us -> 0 us
  between operations: 16.1 us -> 0.64 us
  starting transfers between devices: 9.35 us -> 0 us
  local copies, waits for them, and re-layouts: 1.05 us -> 3.76 us
  other arithmetic: 2.63 us -> 0.66 us
    ppermute x8 -> x0, waiting for transfers between devices: 110 us -> none  [from_behind(): return lax.ppermute(value, axis, pairs)]
    pallas_call x0 -> x1, Pallas kernels: none -> 92.2 us  [fused_body(): pl.pallas_call(functools.partial(fused_kernel, nz), out_shape=[jax.ShapeD...]
    psum x2 -> x0, blocking collectives: 16.3 us -> none  [the longest x1 10.5 us: body(): norm_sq = lax.psum(jnp.sum(values * values), 'samp')]
    dot_general x10 -> x0, matrix products: 15.6 us -> none  [the longest x3 7.87 us: partial_tiles(): lax.dot_general(own_scores, vis_scores, spec, preferred_element_type=jnp....]
    psum x1 -> x0, waiting for transfers between devices: 14.6 us -> none  [kernel_rows(): gram, score_gram = lax.psum((parts[0], parts[1]), ('site', 'sub'))]
    unnamed x1 -> x0, blocking collectives: 9.99 us -> none
    ppermute x8 -> x0, starting transfers between devices: 9.31 us -> none  [from_behind(): return lax.ppermute(value, axis, pairs)]
    unnamed x12 -> x6, local copies, waits for them, and re-layouts: 0.96 us -> 3.76 us
  transfers between devices with their start and end apart: 9 -> 0, of which waited for: 8 -> 0; matrix products, arithmetic and copies ran while one was open for 9% -> 0% of each run, Pallas kernels for 0% -> 0%
where the time goes in v1:
time: 97.4 us; the launch traced here: 97.3 us
  Pallas kernels  92.2 us (95%)
  local copies, waits for them, and re-layouts  3.76 us (4%)
    pallas_call x1, Pallas kernels, fused_body(): pl.pallas_call(functools.partial(fused_kernel, nz), out_shape=[jax.ShapeD...  92.2 us
    unnamed x6, local copies, waits for them, and re-layouts  3.76 us

profile of v1, /device:TPU:0, one launch (start us, length us, event | category | flops | bytes accessed | tf_op | source)
XLA Modules:
  0.0 97.3 jit_solution(7686213207394779878)
XLA Ops:
  0.6 0.7 reshape.19
  1.3 0.0 copy-start
  1.3 1.3 %copy-done = bf16[160,4096]{1,0:T(8,128)(2,1)S(1)} copy-done((bf16[160,4096]{1,0:T(8,128)(2,1)S(1)}, bf16[160,4096]{1,0:T(8,128)(2,1)}, u32[]{:S(2)}) %copy-start) | copy-done | bytes 1310744
  2.6 0.0 copy-start.1
  2.6 1.3 %copy-done.1 = bf16[160,4096]{1,0:T(8,128)(2,1)S(1)} copy-done((bf16[160,4096]{1,0:T(8,128)(2,1)S(1)}, bf16[160,4096]{1,0:T(8,128)(2,1)}, u32[]{:S(2)}) %copy-start.1) | copy-done | bytes 1310744
  3.9 92.2 %shard_map.50 = (f32[1,160]{1,0:T(1,128)S(1)}, f32[1,160]{1,0:T(1,128)S(1)}) custom-call(bf16[160,4096]{1,0:T(8,128)(2,1)S(1)} %copy-done, bf16[160,4096]{1,0:T(8,128)(2,1)S(1)} %copy-done.1, f32[1,160]{1,0:T(1,128)S(1)} %bitcast.5), custom_call_target="tpu_custom_call" | custom-call | flops 1677721600 | bytes 2621440 | tf_op jit(solution)/shard_map/pallas_call | solution.py:410
  96.1 0.6 copy.7
  96.7 0.6 copy.8
Async XLA Ops:
  1.3 1.3 %copy-start = (bf16[160,4096]{1,0:T(8,128)(2,1)S(1)}, bf16[160,4096]{1,0:T(8,128)(2,1)}, u32[]{:S(2)}) copy-start(bf16[160,4096]{1,0:T(8,128)(2,1)} %points.1) | copy-start | bytes 3932164
  2.6 1.3 %copy-start.1 = (bf16[160,4096]{1,0:T(8,128)(2,1)S(1)}, bf16[160,4096]{1,0:T(8,128)(2,1)}, u32[]{:S(2)}) copy-start(bf16[160,4096]{1,0:T(8,128)(2,1)} %scores.1) | copy-start | bytes 3932164

commit v2 on v1

--- a/solution.py
+++ b/solution.py
@@ -90,6 +90,7 @@
 
 MESH = pl.DeviceIdType.MESH
 LANES = 128
+PARTS = 4
 F32 = jnp.float32
 
 
@@ -113,15 +114,12 @@
     points,
     scores,
     target,
-    coeff,
-    residual,
+    result,
     gathered,
     own_points,
     tiles,
     core_in,
-    samp_in,
-    piece,
-    site_in,
+    pieces,
     vec_out,
     vec_in,
     img_out,
@@ -139,19 +137,20 @@
     img_send,
     img_recv,
     core_sem,
-    samp_send,
-    samp_recv,
-    site_sem,
+    piece_send,
+    piece_recv,
 ):
     z = lax.axis_index("samp")
     x = lax.axis_index("site")
     c = lax.axis_index("sub")
     peers = 4 * nz
     me = (c * nz + z) * 2 + x
-    count = target.shape[1]
+    count = target.shape[0]
     total = nz * count
     nb = total // LANES
     span = points.shape[1] // nz
+    parts = gathered.shape[0]
+    sub = span // parts
     share = LANES // 2
     rows = share // nz
     half = rows // 2
@@ -166,21 +165,22 @@
         )
     pl.semaphore_wait(barrier, peers - 1)
 
-    def strip(kind, to):
+    def strip(kind, to, part):
         ref = points if kind == 0 else scores
-        return ref.at[:, pl.ds(pl.multiple_of(span * to, span), span)]
-
-    def slot(source_z, source_x):
+        at = pl.multiple_of(span * to + sub * part, sub)
+        return ref.at[:, pl.ds(at, sub)]
+
+    def slot(source_z, source_x, part):
         return gathered.at[
-            source_x, pl.ds(pl.multiple_of(count * source_z, count), count), :
+            part, source_x, pl.ds(pl.multiple_of(count * source_z, count), count), :
         ]
 
-    def send_data(kind, to, number):
-        return pltpu.make_async_remote_copy(
-            src_ref=strip(kind, to),
-            dst_ref=slot(z, x),
-            send_sem=data_send.at[number],
-            recv_sem=data_recv.at[z, x],
+    def send_data(kind, to, part, number):
+        return pltpu.make_async_remote_copy(
+            src_ref=strip(kind, to, part),
+            dst_ref=slot(z, x, part),
+            send_sem=data_send.at[part, number],
+            recv_sem=data_recv.at[part, z, x],
             device_id={"samp": to, "site": kind},
             device_id_type=MESH,
         )
@@ -189,22 +189,25 @@
     if nz == 4:
         order = [(z + 2) % 4, 3 - z, z + 1 - 2 * (z % 2)]
     sends = []
-    for to in order:
+
+    def same_chip(kind, part):
+        keep = pltpu.make_async_copy(
+            strip(kind, z, part), slot(z, x, part), local_sem.at[1 + part]
+        )
+        give = send_data(1 - kind, z, part, 2 * nz - 2)
+        return keep, give
+
+    for part in range(parts):
+        for n, to in enumerate(order):
+            for kind in (0, 1):
+                sends.append(send_data(kind, to, part, 2 * n + kind))
+                sends[-1].start()
         for kind in (0, 1):
-            sends.append(send_data(kind, to, len(sends)))
-            sends[-1].start()
-
-    def same_chip(kind):
-        keep = pltpu.make_async_copy(strip(kind, z), slot(z, x), local_sem.at[1])
-        give = send_data(1 - kind, z, 2 * nz - 2)
-        return keep, give
-
-    for kind in (0, 1):
-
-        @pl.when(x == kind)
-        def _():
-            for copy in same_chip(kind):
-                copy.start()
+
+            @pl.when(x == kind)
+            def _():
+                for copy in same_chip(kind, part):
+                    copy.start()
 
     fetch = pltpu.make_async_copy(points, own_points, local_sem.at[0])
     fetch.start()
@@ -218,7 +221,7 @@
     eye_row, eye_col = ids(LANES)
     vec_out[...] = jnp.zeros_like(vec_out)
     vec_out[0:1, 0:count] = spread(self_sq, row_ids, col_ids)
-    vec_out[1:2, 0:count] = target[...]
+    vec_out[1:2, 0:count] = target[...].astype(F32).reshape(1, count)
 
     def send_vec(source, to, number):
         return pltpu.make_async_remote_copy(
@@ -233,6 +236,84 @@
     for k in range(1, peers):
         send_vec(me, (me + k) % peers, k - 1).start()
     vec_in[me] = vec_out[...]
+    def arrival(source_z, source_x, part):
+        return pltpu.make_async_remote_copy(
+            src_ref=slot(source_z, source_x, part),
+            dst_ref=slot(source_z, source_x, part),
+            send_sem=data_send.at[part, 0],
+            recv_sem=data_recv.at[part, source_z, source_x],
+            device_id={"samp": source_z, "site": 1 - x},
+            device_id_type=MESH,
+        )
+
+    pairs = [(i, j) for i in range(nb) for j in range(i, nb)]
+    for part in range(parts):
+        pltpu.make_async_copy(
+            slot(z, x, part), slot(z, x, part), local_sem.at[1 + part]
+        ).wait()
+        arrival(z, 1 - x, part).wait_recv()
+        for k in range(1, nz):
+            for j in (0, 1):
+                arrival((z + k) % nz, j, part).wait_recv()
+        for i in range(nb):
+            panel = jnp.zeros((LANES, total - LANES * i), F32)
+            for j in (0, 1):
+                panel = panel + lax.dot_general(
+                    gathered[part, j, LANES * i : LANES * (i + 1), :],
+                    gathered[part, j, LANES * i : total, :],
+                    (((1,), (1,)), ((), ())),
+                    preferred_element_type=F32,
+                )
+            for j in range(i, nb):
+                block = panel[:, LANES * (j - i) : LANES * (j - i + 1)]
+                n = pairs.index((i, j))
+                tiles[n] = block if part == 0 else tiles[n] + block
+
+    mine = pl.ds(pl.multiple_of(share * c, share), share)
+    theirs = pl.ds(pl.multiple_of(share * (1 - c), share), share)
+    to_core = pltpu.make_async_remote_copy(
+        src_ref=tiles.at[:, theirs, :],
+        dst_ref=core_in,
+        send_sem=core_sem.at[0],
+        recv_sem=core_sem.at[1],
+        device_id={"sub": 1 - c},
+        device_id_type=MESH,
+    )
+    to_core.start()
+    to_core.wait_recv()
+    core_in[...] = core_in[...] + tiles[:, mine, :]
+
+    def piece_rows(to_z, to_x):
+        return pl.ds(pl.multiple_of(rows * to_z + half * to_x, half), half)
+
+    def send_piece(to_z, to_x, number):
+        return pltpu.make_async_remote_copy(
+            src_ref=core_in.at[:, piece_rows(to_z, to_x), :],
+            dst_ref=pieces.at[x, z],
+            send_sem=piece_send.at[number],
+            recv_sem=piece_recv.at[x, z],
+            device_id={"samp": to_z, "site": to_x},
+            device_id_type=MESH,
+        )
+
+    def piece_arrival(source_z, source_x):
+        return pltpu.make_async_remote_copy(
+            src_ref=pieces.at[source_x, source_z],
+            dst_ref=pieces.at[source_x, source_z],
+            send_sem=piece_send.at[0],
+            recv_sem=piece_recv.at[source_x, source_z],
+            device_id={"samp": source_z, "site": 1 - x},
+            device_id_type=MESH,
+        )
+
+    piece_sends = []
+    for to in order:
+        for kind in (1 - x, x):
+            piece_sends.append(send_piece(to, kind, len(piece_sends)))
+            piece_sends[-1].start()
+    piece_sends.append(send_piece(z, 1 - x, len(piece_sends)))
+    piece_sends[-1].start()
+    pieces[x, z] = core_in[:, piece_rows(z, x), :]
     for k in range(1, peers):
         send_vec((me + k) % peers, (me + k) % peers, k - 1).wait_recv()
     for k in range(nz):
@@ -250,84 +331,14 @@
         block = pl.ds(b * LANES, LANES)
         norm_row[b : b + 1, :] = spread(norm_col[block, :], eye_row, eye_col)
         value_row[b : b + 1, :] = spread(value_col[block, :], eye_row, eye_col)
-
-    def arrival(source_z, source_x):
-        return pltpu.make_async_remote_copy(
-            src_ref=slot(source_z, source_x),
-            dst_ref=slot(source_z, source_x),
-            send_sem=data_send.at[0],
-            recv_sem=data_recv.at[source_z, source_x],
-            device_id={"samp": source_z, "site": 1 - x},
-            device_id_type=MESH,
-        )
-
-    pltpu.make_async_copy(slot(z, x), slot(z, x), local_sem.at[1]).wait()
-    arrival(z, 1 - x).wait_recv()
+    piece_arrival(z, 1 - x).wait_recv()
     for k in range(1, nz):
         for j in (0, 1):
-            arrival((z + k) % nz, j).wait_recv()
-
-    pairs = [(i, j) for i in range(nb) for j in range(i, nb)]
-    for i in range(nb):
-        panel = jnp.zeros((LANES, total - LANES * i), F32)
-        for j in (0, 1):
-            panel = panel + lax.dot_general(
-                gathered[j, LANES * i : LANES * (i + 1), :],
-                gathered[j, LANES * i : total, :],
-                (((1,), (1,)), ((), ())),
-                preferred_element_type=F32,
-            )
-        for j in range(i, nb):
-            tiles[pairs.index((i, j))] = panel[:, LANES * (j - i) : LANES * (j - i + 1)]
-
-    mine = pl.ds(pl.multiple_of(share * c, share), share)
-    theirs = pl.ds(pl.multiple_of(share * (1 - c), share), share)
-    to_core = pltpu.make_async_remote_copy(
-        src_ref=tiles.at[:, theirs, :],
-        dst_ref=core_in,
-        send_sem=core_sem.at[0],
-        recv_sem=core_sem.at[1],
-        device_id={"sub": 1 - c},
-        device_id_type=MESH,
-    )
-    to_core.start()
-    to_core.wait_recv()
-    core_in[...] = core_in[...] + tiles[:, mine, :]
-
-    def send_piece(source, to, number):
-        return pltpu.make_async_remote_copy(
-            src_ref=core_in.at[:, pl.ds(pl.multiple_of(rows * to, rows), rows), :],
-            dst_ref=samp_in.at[source],
-            send_sem=samp_send.at[number],
-            recv_sem=samp_recv.at[source],
-            device_id={"samp": to},
-            device_id_type=MESH,
-        )
-
-    for number, to in enumerate(order):
-        send_piece(z, to, number).start()
-    samp_in[z] = core_in[:, pl.ds(pl.multiple_of(rows * z, rows), rows), :]
+            piece_arrival((z + k) % nz, j).wait_recv()
+    gram, score_gram = pieces[0, 0], pieces[1, 0]
     for k in range(1, nz):
-        send_piece((z + k) % nz, (z + k) % nz, 0).wait_recv()
-    summed = samp_in[0]
-    for k in range(1, nz):
-        summed = summed + samp_in[k]
-    piece[...] = summed
-
-    to_site = pltpu.make_async_remote_copy(
-        src_ref=piece.at[:, pl.ds(pl.multiple_of(half * (1 - x), half), half), :],
-        dst_ref=site_in,
-        send_sem=site_sem.at[0],
-        recv_sem=site_sem.at[1],
-        device_id={"site": 1 - x},
-        device_id_type=MESH,
-    )
-    to_site.start()
-    to_site.wait_recv()
-    here = piece[:, pl.ds(pl.multiple_of(half * x, half), half), :]
-    there = site_in[...]
-    gram = jnp.where(x == 0, here, there)
-    score_gram = jnp.where(x == 0, there, here)
+        gram = gram + pieces[0, k]
+        score_gram = score_gram + pieces[1, k]
 
     width = float(SITES)
     lane = lax.broadcasted_iota(jnp.int32, (half, LANES), 1)
@@ -382,19 +393,19 @@
     alpha = norm_sq / curvature
     own = image_col[pl.ds(pl.multiple_of(count * z, count), count), 0:1]
     own_image = spread(own, row_ids, col_ids)
-    coeff[...] = alpha * target[...]
-    residual[...] = target[...] - alpha * own_image
+    result[0:1, :] = own_image
+    result[1:2, :] = jnp.broadcast_to(alpha, (1, count))
 
     for copy in sends:
         copy.wait_send()
-    send_data(0, z, 2 * nz - 2).wait_send()
+    for part in range(parts):
+        send_data(0, z, part, 2 * nz - 2).wait_send()
     for k in range(1, peers):
         send_vec(me, (me + k) % peers, k - 1).wait_send()
         send_img(me, (me + k) % peers, k - 1).wait_send()
     to_core.wait_send()
-    to_site.wait_send()
-    for number, to in enumerate(order):
-        send_piece(z, to, number).wait_send()
+    for copy in piece_sends:
+        copy.wait_send()
 
 
 def fused_body(nz, points, scores, target):
@@ -402,24 +413,23 @@
     total = nz * count
     nb = total // LANES
     blocks = nb * (nb + 1) // 2
+    parts = PARTS
     rows = LANES // 2 // nz
     peers = 4 * nz
     dma = pltpu.SemaphoreType.DMA
     vmem = pl.BlockSpec(memory_space=pltpu.VMEM)
     wide = -(-count // LANES) * LANES
-    coeff, residual = pl.pallas_call(
+    result = pl.pallas_call(
         functools.partial(fused_kernel, nz),
-        out_shape=[jax.ShapeDtypeStruct((1, count), F32)] * 2,
+        out_shape=jax.ShapeDtypeStruct((2, count), F32),
         in_specs=[pl.BlockSpec(memory_space=pl.ANY)] * 2 + [vmem],
-        out_specs=[vmem, vmem],
+        out_specs=vmem,
         scratch_shapes=[
-            pltpu.VMEM((2, total, sites // nz), points.dtype),
+            pltpu.VMEM((parts, 2, total, sites // nz // parts), points.dtype),
             pltpu.VMEM((count, sites), points.dtype),
             pltpu.VMEM((blocks, LANES, LANES), F32),
             pltpu.VMEM((blocks, LANES // 2, LANES), F32),
-            pltpu.VMEM((nz, blocks, rows, LANES), F32),
-            pltpu.VMEM((blocks, rows, LANES), F32),
-            pltpu.VMEM((blocks, rows // 2, LANES), F32),
+            pltpu.VMEM((2, nz, blocks, rows // 2, LANES), F32),
             pltpu.VMEM((8, wide), F32),
             pltpu.VMEM((peers, 8, wide), F32),
             pltpu.VMEM((16, LANES), F32),
@@ -429,28 +439,29 @@
             pltpu.VMEM((total, LANES), F32),
             pltpu.VMEM((8, LANES), F32),
             pltpu.VMEM((8, LANES), F32),
-            dma((2,)),
-            dma((2 * nz - 1,)),
-            dma((nz, 2)),
+            dma((1 + parts,)),
+            dma((parts, 2 * nz - 1)),
+            dma((parts, nz, 2)),
             dma((peers - 1,)),
             dma((peers,)),
             dma((peers - 1,)),
             dma((peers,)),
             dma((2,)),
-            dma((nz - 1,)),
-            dma((nz,)),
-            dma((2,)),
+            dma((2 * nz - 1,)),
+            dma((2, nz)),
         ],
         compiler_params=pltpu.CompilerParams(
-            collective_id=0, has_side_effects=True, vmem_limit_bytes=40 * 2**20
+            collective_id=0, has_side_effects=True, vmem_limit_bytes=56 * 2**20
         ),
         cost_estimate=pl.CostEstimate(
             flops=2 * total * total * sites // 2,
             bytes_accessed=4 * count * sites,
             transcendentals=0,
         ),
-    )(points, scores, target.astype(F32).reshape(1, count))
-    return coeff.reshape(count), residual.reshape(count)
+    )(points, scores, target)
+    values = target.astype(F32)
+    image, alpha = result[0], result[1]
+    return alpha * values, values - alpha * image
 
 
 def solution(mesh):
@@ -466,7 +477,7 @@
             and points.shape[0] % 16 == 0
             and total % LANES == 0
             and total <= 8 * LANES
-            and points.shape[1] % (nz * LANES) == 0
+            and points.shape[1] % (nz * PARTS * LANES) == 0
             and points.shape[1] % 512 == 0
         )
         if fits:

time: 97.4 us -> 89.3 us (0.917)
  Pallas kernels: 92.2 us -> 87.1 us
  local copies, waits for them, and re-layouts: 3.76 us -> 0.75 us
    pallas_call x1, Pallas kernels: 92.2 us -> 87.1 us  [fused_body(): pl.pallas_call(functools.partial(fused_kernel, nz), out_shape=jax.ShapeDt...]
    unnamed x6 -> x2, local copies, waits for them, and re-layouts: 3.76 us -> 0.01 us
where the time goes in v2:
time: 89.3 us; the launch traced here: 89.1 us
  Pallas kernels  87.1 us (98%)
    pallas_call x1, Pallas kernels, fused_body(): pl.pallas_call(functools.partial(fused_kernel, nz), out_shape=jax.ShapeDt...  87.1 us

profile of v2, /device:TPU:0, one launch (start us, length us, event | category | flops | bytes accessed | tf_op | source)
XLA Modules:
  0.0 89.1 jit_solution(11636681893592563978)
XLA Ops:
  0.6 0.0 copy-start
  0.6 87.1 %shard_map.50 = f32[2,160]{1,0:T(2,128)} custom-call(bf16[160,4096]{1,0:T(8,128)(2,1)} %points.1, bf16[160,4096]{1,0:T(8,128)(2,1)} %scores.1, bf16[160]{0:T(256)(128)(2,1)} %target.1), custom_call_target="tpu_custom_call" | custom-call | flops 1677721600 | bytes 2621440 | tf_op jit(solution)/shard_map/pallas_call | solution.py:422
  87.8 0.7 fusion
  88.5 0.0 copy-done
  88.5 0.6 convert_subtract_fusion
Async XLA Ops:
  0.6 87.9 %copy-start = (bf16[160]{0:T(256)(128)(2,1)S(1)}, bf16[160]{0:T(256)(128)(2,1)}, u32[]{:S(2)}) copy-start(bf16[160]{0:T(256)(128)(2,1)} %target.1) | copy-start | bytes 964
